TPU v7x, 256 devices: a whole 4x4x8 slice. The times are simulated.
256 devices in a mesh: tm: 8 (over x, core), seq: 32 (over y, z).
Axes of the slice: x: 4, y: 4, z: 8, core: 2. Of those that a mesh axis runs over, the one named last changes fastest.
Arguments:
- projected: bfloat16 [8, 4096, 3, 4096], P('tm', 'seq'), may hold values from -16 to 16
- scale_table: float32 [8, 3, 32], replicated, may hold values from 0.8 to 1.25
- group_index: int32 [8], P('tm'), may hold values from 0 to 7
- timesteps: int32 [8], P('tm'), may hold values from 1 to 999, as said below
- time_weight: bfloat16 [256, 2, 4096], replicated, may hold values from -0.375 to 0.375
- head_weight: bfloat16 [64, 4096], replicated, may hold values from -0.09375 to 0.09375
- start_latent: float32 [2048, 128], P('seq'), may hold values from -3 to 3
Outputs:
- latents: float32 [8, 2048, 128], P('tm', 'seq')
Inputs may be any that keep to these rules, and one draw needn't show every extreme that they name: `timesteps`: strictly decreasing along the steps.
All inputs are finite; a program needn't handle non-finite values.
Results may differ from a plain program's by a relative error of at most 0.0026.
Values may be sent and summed in bfloat16 or wider, within the bound.
A program may use at most 64 MiB of HBM per device.

v0:
```python
import math

import jax
import jax.numpy as jnp
from jax import lax
from jax.sharding import PartitionSpec as P


def passed_along(block, axis, distance):
    devices = range(lax.axis_size(axis))
    route = [(i - distance, i) for i in devices if i - distance in devices]
    return lax.ppermute(block, axis, route)


def entering(x, axis, combine, identity):
    peers, mine = (lax.axis_size(axis), lax.axis_index(axis))
    everything = lax.all_gather(x, axis)
    start = jnp.broadcast_to(jnp.asarray(identity, x.dtype), x.shape)

    def lap(k, before):
        reached = k < mine
        new = combine(before, everything[k])
        return jnp.where(reached, new, before)

    return lax.fori_loop(0, peers, lap, start)


def sinusoid(times, freq_dim):
    half_freq = freq_dim // 2
    frequencies = jnp.power(
        jnp.float32(10000.0), -jnp.arange(half_freq, dtype=jnp.float32) / half_freq
    )
    angles = times.astype(jnp.float32)[:, None] * frequencies[None, :]
    return jnp.concatenate([jnp.cos(angles), jnp.sin(angles)], axis=1)


def modulate(outputs, shift_part, scale_part, center, inverse):
    return (
        (outputs.astype(jnp.float32) - center) * inverse * (1.0 + scale_part) + shift_part
    ).astype(jnp.bfloat16)


def combine(earlier_part, later_part):
    return earlier_part + later_part


def body(projected, scale_table, group_index, timesteps, time_weight, head_weight, start_latent):
    width = projected.shape[3]
    freq_dim = time_weight.shape[0]
    head_total = scale_table.shape[2]
    head_size = width // head_total
    seq_devices = lax.axis_size("seq")
    head_local = head_total // seq_devices
    local_width = head_local * head_size
    seq_index = lax.axis_index("seq")
    latent_dim = head_weight.shape[0]
    later_time = passed_along(timesteps, "tm", -1)
    step_size = ((later_time - timesteps).astype(jnp.float32) / 1000.0)[0]
    embedded = sinusoid(timesteps, freq_dim).astype(jnp.bfloat16)
    modulation = jnp.dot(
        embedded, time_weight.reshape(freq_dim, 2 * width), preferred_element_type=jnp.float32
    )
    shift_all = modulation[:, :width]
    scale_all = modulation[:, width:]
    group_mask = jnp.arange(scale_table.shape[0])[:, None, None] == group_index[0]
    table_row = jnp.sum(jnp.where(group_mask, scale_table, 0.0), axis=0)
    own_scales = lax.dynamic_slice_in_dim(table_row, seq_index * head_local, head_local, 1)
    factor = own_scales[0] * own_scales[1] / math.sqrt(head_size)
    value_scale = own_scales[2]
    block = lax.all_to_all(projected, "seq", split_axis=3, concat_axis=1, tiled=True)
    item_total = block.shape[0]
    length = block.shape[1]
    coded = block.reshape(item_total, length, 3, head_local, head_size)
    query_all = coded[:, :, 0]
    key_codes = coded[:, :, 1]
    value_codes = coded[:, :, 2]
    block_rows = 512

    def one_block(first_row):
        query_part = lax.dynamic_slice_in_dim(query_all, first_row, block_rows, 1)
        scores = (
            jnp.einsum("nqhd,nkhd->nhqk", query_part, key_codes, preferred_element_type=jnp.float32)
            * factor[None, :, None, None]
        )
        row_max = jnp.max(scores, axis=-1, keepdims=True)
        weights = jnp.exp(scores - row_max)
        row_sum = jnp.sum(weights, axis=-1, keepdims=True)
        blended = jnp.einsum(
            "nhqk,nkhd->nqhd",
            weights.astype(jnp.bfloat16),
            value_codes,
            preferred_element_type=jnp.float32,
        )
        ratio = value_scale[None, :, None, None] / row_sum
        return (blended * ratio.transpose(0, 2, 1, 3)).astype(jnp.bfloat16)

    pieces = lax.map(one_block, jnp.arange(length // block_rows) * block_rows)
    attended = pieces.transpose(1, 0, 2, 3, 4).reshape(item_total, length, local_width)
    gathered = lax.all_to_all(attended, "seq", split_axis=1, concat_axis=2, tiled=True)[0]
    as_float = gathered.astype(jnp.float32)
    center = jnp.mean(as_float, axis=-1, keepdims=True)
    spread = jnp.mean(jnp.square(as_float - center), axis=-1, keepdims=True)
    normed = modulate(gathered, shift_all, scale_all, center, lax.rsqrt(spread + 1e-06))
    velocity = lax.dot_general(
        normed, head_weight, (((1,), (1,)), ((), ())), preferred_element_type=jnp.float32
    )
    velocity = velocity.reshape(velocity.shape[0] // 2, 2 * latent_dim)
    drift = step_size * velocity
    earlier = entering(drift, "tm", combine, jnp.zeros_like(drift))
    summed = earlier + drift
    return (start_latent + summed)[None]


def solution(mesh):
    placed = (P("tm", "seq", None, None), P(), P("tm"), P("tm"), P(), P(), P("seq", None))
    return jax.shard_map(
        body, mesh=mesh, in_specs=placed, out_specs=P("tm", "seq", None), check_vma=False
    )
```

profile of v0, /device:TPU:7, one launch (start us, length us, event | category | flops | bytes accessed | tf_op | source)
XLA Modules:
  0.0 283.1 jit_solution(5060592392441792060)
XLA Ops:
  0.0 7.2 %copy.29 = bf16[1,128,3,4096]{1,2,0,3:T(4,128)(2,1)} copy(bf16[1,128,3,4096]{3,1,2,0:T(8,128)(2,1)} %param.11) | data formatting | bytes 6291456 | tf_op args[0]
  7.2 11.5 %all-to-all-start = ((bf16[1,128,3,4096]{1,2,0,3:T(4,128)(2,1)}), bf16[1,128,3,4096]{1,2,0,3:T(4,128)(2,1)}, u32[]{:S(2)}, u32[]{:S(2)}) async-start(bf16[1,128,3,4096]{1,2,0,3:T(4,128)(2,1)} %copy.29), calls=%async_computation | async-start | bytes 8388608 | tf_op jit(solution)/shard_map/all_to_all | solution.py:70
  21.5 90.0 %all-to-all-done = bf16[1,128,3,4096]{1,2,0,3:T(4,128)(2,1)} async-done(((bf16[1,128,3,4096]{1,2,0,3:T(4,128)(2,1)}), bf16[1,128,3,4096]{1,2,0,3:T(4,128)(2,1)}, u32[]{:S(2)}, u32[]{:S(2)}) %all-to-all-start) | async-done | bytes 3145760 | tf_op jit(solution)/shard_map/all_to_all | solution.py:70
  111.5 7.1 %copy.30 = bf16[1,128,3,32,128]{4,1,3,2,0:T(8,128)(2,1)} copy(bf16[1,128,3,32,128]{1,2,4,3,0:T(4,128)(2,1)} %bitcast.11) | data formatting | bytes 6291456 | tf_op jit(solution)/shard_map/all_to_all | solution.py:70
  118.6 3.0 %slice_bitcast_fusion = (bf16[1,4096,1,128]{3,1,2,0:T(8,128)(2,1)}, bf16[1,4096,1,128]{3,1,2,0:T(8,128)(2,1)S(1)}, bf16[1,4096,1,128]{3,1,2,0:T(8,128)(2,1)S(1)}) fusion(bf16[1,4096,3,1,128]{4,1,3,2,0:T(8,128)(2,1)} %bitcast.105), kind=kLoop, calls=%fused_computation.24 | loop fusion | bytes 6291456 | tf_op jit(solution)/shard_map/squeeze | solution.py:76
  121.6 66.9 %while.24 = (s32[]{:T(128)}, bf16[8,1,512,1,128]{4,2,3,1,0:T(8,128)(2,1)}, s32[8]{0:T(128)S(1)}, bf16[1,4096,1,128]{3,1,2,0:T(8,128)(2,1)S(1)}, bf16[1,4096,1,12...) while((s32[]{:T(128)}, ...), condition=%wide.region_4.5_spmd, body=%wide.region_1.4_spmd.sunk | while | flops 1090649600 | bytes 31734984 | solution.py:97
  127.9 2.1 fusion.43
  144.6 2.1 fusion.43
  153.0 2.1 fusion.43
  161.3 2.1 fusion.43
  169.7 2.1 fusion.43
  178.1 2.1 fusion.43
  186.4 2.1 fusion.43
  188.5 3.2 %copy.41 = bf16[1,4096,128]{2,0,1:T(2,128)(2,1)S(1)} copy(bf16[1,4096,128]{2,1,0:T(8,128)(2,1)} %bitcast.20) | data formatting | bytes 2097152 | tf_op jit(solution)/shard_map/reshape;transpose | solution.py:98
  192.2 23.4 %reduce.10 = bf16[4096,128]{1,0:T(8,128)(2,1)} reduce(bf16[4096,1,128]{2,1,0:T(2,128)(2,1)S(1)} %bitcast.106, bf16[]{:T(256)} %broadcast.85), dimensions={1}, to_apply=%bitcast.80.reduce_sub_computation | reduce | bytes 2097154
  215.6 2.1 reshape.119
  217.7 9.2 %all-to-all-start.1 = ((bf16[32,2,8192]{2,1,0:T(2,128)(2,1)}), bf16[32,2,8192]{2,1,0:T(2,128)(2,1)S(1)}, u32[]{:S(2)}, u32[]{:S(2)}) async-start(bf16[32,2,8192]{2,1,0:T(2,128)(2,1)} %reshape.119), calls=%async_computation.1 | async-start | bytes 2097152 | tf_op jit(solution)/shard_map/all_to_all | solution.py:99
  227.0 3.6 %collective-permute-start = (s32[1]{0:T(128)}, s32[1]{0:T(128)}, u32[]{:S(2)}, u32[]{:S(2)}) collective-permute-start(s32[1]{0:T(128)} %param.14), channel_id=1, source_target_pairs={{32,0},{64,32},{96,64},{128,96},{160,128},{192,160},{224,192},{33,... | collective-permute-start | bytes 20 | tf_op jit(solution)/shard_map/ppermute | solution.py:12
  231.3 8.6 %copy.36 = bf16[32,8,2,4096]{3,1,2,0:T(8,128)(2,1)} copy(bf16[32,8,2,4096]{3,2,1,0:T(2,128)(2,1)} %bitcast.107) | data formatting | bytes 8388608
  239.9 2.8 %fusion.31 = f32[1,8192]{1,0:T(1,128)S(1)} fusion(bf16[256,1]{0,1:T(2,128)(2,1)S(1)} %reshape.117, bf16[256,8192]{1,0:T(8,128)(2,1)} %bitcast.104), kind=kOutput, calls=%fused_computation.45 | convolution fusion | flops 4194304 | bytes 4227584 | tf_op jit(solution)/shard_map/dot_general | solution.py:60
  243.4 8.2 %all-to-all-done.1 = bf16[32,2,8192]{2,1,0:T(2,128)(2,1)S(1)} async-done(((bf16[32,2,8192]{2,1,0:T(2,128)(2,1)}), bf16[32,2,8192]{2,1,0:T(2,128)(2,1)S(1)}, u32[]{:S(2)}, u32[]{:S(2)}) %all-to-all-start.1) | async-done | bytes 1048608 | tf_op jit(solution)/shard_map/all_to_all | solution.py:99
  251.6 3.5 %reshape.120 = bf16[4096,1,128]{2,1,0:T(2,128)(2,1)} reshape(bf16[32,2,8192]{2,1,0:T(2,128)(2,1)S(1)} %all-to-all-done.1) | data formatting | bytes 2097152
  260.2 3.7 %fusion.28 = bf16[128,4096]{0,1:T(8,128)(2,1)S(1)} fusion(f32[1,128,32,128]{1,3,2,0:T(8,128)} %copy.33, f32[4096]{0:T(1024)S(1)} %bitcast.109, f32[4096]{0:T(1024)S(1)} %bitcast.108, f32[128]{0:T(128)S(1)} %add_rsqrt_fusion, f32[128]{0:T(128)S(1)} %broadcast_multiply_fusion.1), kind=kLoop, calls=%fused_computation.22 | loop fusion | flops 2621440 | bytes 3179520 | tf_op jit(solution)/shard_map/convert_element_type | solution.py:40
  264.5 17.7 %all_gather.4 = f32[8,64,128]{2,1,0:T(8,128)S(1)} all-gather(f32[1,64,128]{2,1,0:T(8,128)S(1)} %mul.91), channel_id=1, replica_groups=mesh['tm'=8,'seq'=32] {'tm'}, dimensions={0}, use_global_device_ids=true | all-gather | bytes 294912 | tf_op jit(solution)/shard_map/all_gather | solution.py:17
  (91 shorter events, 43.4 us)
Async XLA Ops:
  0.0 263.9 %copy-start = (bf16[64,4096]{1,0:T(8,128)(2,1)S(1)}, bf16[64,4096]{1,0:T(8,128)(2,1)}, u32[]{:S(2)}) copy-start(bf16[64,4096]{1,0:T(8,128)(2,1)} %param.16) | copy-start | bytes 1572868
  7.2 12.2 %copy-start.4 = (f32[8,3,32]{2,0,1:T(8,128)S(1)}, f32[8,3,32]{2,0,1:T(8,128)}, u32[]{:S(2)}) copy-start(f32[8,3,32]{2,0,1:T(8,128)} %param.12) | copy-start | bytes 9220
  7.2 104.2 %all-to-all-start = ((bf16[1,128,3,4096]{1,2,0,3:T(4,128)(2,1)}), bf16[1,128,3,4096]{1,2,0,3:T(4,128)(2,1)}, u32[]{:S(2)}, u32[]{:S(2)}) async-start(bf16[1,128,3,4096]{1,2,0,3:T(4,128)(2,1)} %copy.29), calls=%async_computation | async-start | bytes 8388608 | tf_op jit(solution)/shard_map/all_to_all | solution.py:70
  125.7 2.1 copy-start.2
  134.1 2.1 copy-start.2
  142.4 2.1 copy-start.2
  150.8 2.1 copy-start.2
  159.2 2.1 copy-start.2
  167.5 2.1 copy-start.2
  175.9 2.1 copy-start.2
  184.3 2.1 copy-start.2
  217.7 33.9 %all-to-all-start.1 = ((bf16[32,2,8192]{2,1,0:T(2,128)(2,1)}), bf16[32,2,8192]{2,1,0:T(2,128)(2,1)S(1)}, u32[]{:S(2)}, u32[]{:S(2)}) async-start(bf16[32,2,8192]{2,1,0:T(2,128)(2,1)} %reshape.119), calls=%async_computation.1 | async-start | bytes 2097152 | tf_op jit(solution)/shard_map/all_to_all | solution.py:99
  227.0 15.8 %collective-permute-start = (s32[1]{0:T(128)}, s32[1]{0:T(128)}, u32[]{:S(2)}, u32[]{:S(2)}) collective-permute-start(s32[1]{0:T(128)} %param.14), channel_id=1, source_target_pairs={{32,0},{64,32},{96,64},{128,96},{160,128},{192,160},{224,192},{33,... | collective-permute-start | bytes 20 | tf_op jit(solution)/shard_map/ppermute | solution.py:12
  255.1 2.2 copy-start.1
  258.3 24.2 %copy-start.3 = (f32[64,128]{1,0:T(8,128)S(1)}, f32[64,128]{1,0:T(8,128)}, u32[]{:S(2)}) copy-start(f32[64,128]{1,0:T(8,128)} %param.17) | copy-start | bytes 98308
where the time goes:
time: 285 us; the launch traced here: 283 us
  waiting for transfers between devices  98.2 us (34%)
  other arithmetic  47.9 us (17%)
  local copies, waits for them, and re-layouts  43.7 us (15%)
  matrix products  30.9 us (11%)
  starting transfers between devices  24.3 us (9%)
  blocking collectives  17.7 us (6%)
  loops' own time  17 us (6%)
  between operations  3.43 us (1%)
    all_to_all x1, waiting for transfers between devices, body(): lax.all_to_all(projected, 'seq', split_axis=3, concat_axis=1, tiled=True)  90 us
    unnamed x2, other arithmetic  23.4 us
    unnamed x13, local copies, waits for them, and re-layouts  22.3 us
    all_gather x1, blocking collectives, entering(): everything = lax.all_gather(x, axis)  17.7 us
    dot_general x8, matrix products, one_block(): jnp.einsum('nhqk,nkhd->nqhd', weights.astype(jnp.bfloat16), value_codes,...  16.8 us
    another operation x1, loops' own time, body(): pieces = lax.map(one_block, jnp.arange(length // block_rows) * block_rows)  16.8 us
    reduce_sum x8, other arithmetic, one_block(): row_sum = jnp.sum(weights, axis=-1, keepdims=True)  11.9 us
    all_to_all x1, starting transfers between devices, body(): lax.all_to_all(projected, 'seq', split_axis=3, concat_axis=1, tiled=True)  11.5 us
  transfers between devices with their start and end apart: 3, of which 2 were waited for; matrix products, arithmetic and copies ran while one was open for 4% of the time, Pallas kernels for 0%

commit v1 on v0

v1 whole, which is shorter than its diff:
```python
import functools
import math

import jax
import jax.numpy as jnp
import numpy as np
from jax import lax
from jax.experimental import pallas as pl
from jax.experimental.pallas import tpu as pltpu
from jax.sharding import PartitionSpec as P

MESH = pl.DeviceIdType.MESH
F32 = jnp.float32
BF16 = jnp.bfloat16

NY, NZ, TM = 4, 8, 8
SEQ = NY * NZ
TOK = 128
HEAD = 128
LAT = 64
KEYS = SEQ * TOK
WIDTH = SEQ * HEAD
FREQ = 256
ROWS = 256
KEY_CHUNK = 512
PACK = 72


def group_dz(g):
    odd = g % 2
    return (4 + odd * ((g + 1) // 2) - (1 - odd) * (g // 2)) % NZ


def group_dy(i):
    return (i + 1) % NY


def kernel(
    proj,
    scale_table,
    group_index,
    timesteps,
    freqs,
    time_weight,
    head_weight,
    start_latent,
    out,
    qbuf,
    kvbuf,
    ktbuf,
    sbuf,
    wblk,
    tw,
    hw,
    consts,
    pbuf,
    ybuf,
    zsend,
    zbuf,
    tsend,
    tbuf,
    later,
    lat,
    kv_send,
    kv_recv,
    q_send,
    q_recv,
    y_send,
    y_recv,
    z_send,
    z_recv,
    t_send,
    t_recv,
    misc,
):
    tm = lax.axis_index("tm")
    me = lax.axis_index("seq")
    my, mz = me // NZ, me % NZ

    def seq_at(dy, dz):
        return ((my + dy + NY) % NY) * NZ + (mz + dz + NZ) % NZ

    def peer(dy, dz):
        return (tm, seq_at(dy, dz))

    cols = pl.ds(pl.multiple_of(me * HEAD, HEAD), HEAD)
    own_codes = pltpu.make_async_copy(proj.at[1:3, :, cols], kvbuf.at[SEQ - 1], misc.at[0])
    own_query = pltpu.make_async_copy(proj.at[0, :, cols], qbuf.at[SEQ - 1], misc.at[1])
    get_tw = pltpu.make_async_copy(time_weight.at[:, :, cols], tw, misc.at[2])
    get_hw = pltpu.make_async_copy(head_weight.at[:, cols], hw, misc.at[3])
    own_codes.start()
    own_query.start()
    get_tw.start()
    get_hw.start()

    barrier = pltpu.get_barrier_semaphore()

    def greet(o, _):
        pl.semaphore_signal(barrier, inc=1, device_id=(tm, (me + o) % SEQ), device_id_type=MESH)
        return 0

    def greet_tm(o, _):
        pl.semaphore_signal(barrier, inc=1, device_id=((tm + o) % TM, me), device_id_type=MESH)
        return 0

    with jax.named_scope("barrier"):
        lax.fori_loop(1, SEQ, greet, 0)
        lax.fori_loop(1, TM, greet_tm, 0)
        pl.semaphore_wait(barrier, SEQ + TM - 2)

    def kv_copy(j):
        g, i = j // NY, j % NY
        to = seq_at(-group_dy(i), -group_dz(g))
        lanes = pl.ds(pl.multiple_of(to * HEAD, HEAD), HEAD)
        return pltpu.make_async_remote_copy(
            src_ref=proj.at[1:3, :, lanes],
            dst_ref=kvbuf.at[j],
            send_sem=kv_send.at[j],
            recv_sem=kv_recv.at[j],
            device_id=(tm, to),
            device_id_type=MESH,
        )

    def q_copy(j):
        g, i = j // NY, j % NY
        to = seq_at(-group_dy(i), -group_dz(g))
        lanes = pl.ds(pl.multiple_of(to * HEAD, HEAD), HEAD)
        return pltpu.make_async_remote_copy(
            src_ref=proj.at[0, :, lanes],
            dst_ref=qbuf.at[j],
            send_sem=q_send.at[j],
            recv_sem=q_recv.at[j],
            device_id=(tm, to),
            device_id_type=MESH,
        )

    def start_kv(j, _):
        kv_copy(j).start()
        return 0

    def start_q(j, _):
        q_copy(j).start()
        return 0

    with jax.named_scope("send"):
        lax.fori_loop(0, SEQ - 1, start_kv, 0)
        lax.fori_loop(0, SEQ - 1, start_q, 0)

    time_copy = pltpu.make_async_remote_copy(
        src_ref=later.at[0],
        dst_ref=later.at[1],
        send_sem=misc.at[4],
        recv_sem=misc.at[5],
        device_id=((tm + TM - 1) % TM, me),
        device_id_type=MESH,
    )
    time_now = jnp.full((8, 128), timesteps[0], jnp.int32).astype(F32)
    later[0] = time_now

    @pl.when(tm > 0)
    def _():
        time_copy.start()

    with jax.named_scope("constants"):
        lane = lax.broadcasted_iota(jnp.int32, (8, 128), 1)
        row = lax.broadcasted_iota(jnp.int32, (8, 128), 0)
        head_lane = lax.broadcasted_iota(jnp.int32, (8, SEQ), 1)
        group_row = lax.broadcasted_iota(jnp.int32, (8, SEQ), 0)
        chosen = (head_lane == me) & (group_row == group_index[0])

        def pick(k):
            kept = jnp.where(chosen, scale_table[k], 0.0)
            return jnp.sum(jnp.sum(kept, axis=1, keepdims=True), axis=0, keepdims=True)

        factor = pick(0) * pick(1) / math.sqrt(HEAD)
        score_scale = factor * math.log2(math.e)
        value_scale = pick(2)

        angles = time_now[0:1, 0:1] * freqs[...]
        wide_lane = lax.broadcasted_iota(jnp.int32, (8, 2 * FREQ), 1)
        wide_row = lax.broadcasted_iota(jnp.int32, (8, 2 * FREQ), 0)
        waves = jnp.where(wide_lane < FREQ, jnp.cos(angles), jnp.sin(angles))
        waves = jnp.where(wide_lane % 2 == wide_row, waves, 0.0).astype(BF16)
        get_tw.wait()
        get_hw.wait()
        modulation = jnp.dot(waves, tw[...].reshape(2 * FREQ, HEAD), preferred_element_type=F32)
        shift, scale = modulation[0:1], modulation[1:2]
        weight = hw[...].astype(F32)
        weight = jnp.concatenate([weight, weight], axis=0)
        scaled = (weight * (1.0 + scale)).T
        shifted = jnp.sum((weight * shift).T, axis=0, keepdims=True)
        high = scaled.astype(BF16)
        low = (scaled - high.astype(F32)).astype(BF16)
        left = lax.broadcasted_iota(jnp.int32, (HEAD, 128), 1) < LAT
        zero = jnp.zeros_like(high)
        wblk[0:HEAD, 0:128] = jnp.where(left, high, zero)
        wblk[0:HEAD, 128:256] = jnp.where(left, low, zero)
        wblk[HEAD : 2 * HEAD, 0:128] = jnp.where(left, zero, high)
        wblk[HEAD : 2 * HEAD, 128:256] = jnp.where(left, zero, low)
        summed = jnp.sum(high.astype(F32) + low.astype(F32), axis=0, keepdims=True)
        consts[...] = jnp.where(row == 2, summed, jnp.where(row == 3, shifted, 0.0))

    own_codes.wait()
    ktbuf[:, KEYS - TOK : KEYS] = kvbuf[SEQ - 1, 0].T

    def take_kv(j, _):
        kv_copy(j).wait_recv()
        ktbuf[:, pl.ds(pl.multiple_of(j * TOK, TOK), TOK)] = kvbuf[j, 0].T
        return 0

    with jax.named_scope("keys"):
        lax.fori_loop(0, SEQ - 1, take_kv, 0)

    def y_copy(g, i):
        return pltpu.make_async_remote_copy(
            src_ref=pbuf.at[g * NY + i],
            dst_ref=ybuf.at[g * NY + i],
            send_sem=y_send.at[g * NY + i],
            recv_sem=y_recv.at[g * NY + i],
            device_id=peer(group_dy(i), 0),
            device_id_type=MESH,
        )

    def z_copy(g):
        return pltpu.make_async_remote_copy(
            src_ref=zsend.at[g],
            dst_ref=zbuf.at[g],
            send_sem=z_send.at[g],
            recv_sem=z_recv.at[g],
            device_id=peer(0, group_dz(g)),
            device_id_type=MESH,
        )

    def join_y(g):
        total = pbuf[g * NY + NY - 1]
        for i in range(NY - 1):
            y_copy(g, i).wait_recv()
            total = total + ybuf[g * NY + i]
        zsend[g] = total

    keys_of = lambda c: slice(c * KEY_CHUNK, (c + 1) * KEY_CHUNK)
    chunks = KEYS // KEY_CHUNK
    ones = jnp.ones((KEY_CHUNK, 128), BF16)
    stat_row = lax.broadcasted_iota(jnp.int32, (16, 3 * HEAD), 0)
    stat_lane = lax.broadcasted_iota(jnp.int32, (16, 3 * HEAD), 1)
    picker = jnp.where(
        ((stat_row == 0) & (stat_lane < HEAD)) | ((stat_row == 1) & (stat_lane >= HEAD)), 1.0, 0.0
    ).astype(BF16)

    def attend(first):
        query = qbuf[pl.ds(first, 2)].reshape(ROWS, HEAD).astype(F32) * score_scale
        high = query.astype(BF16)
        low = (query - high.astype(F32)).astype(BF16)
        both = jnp.concatenate([high, low], axis=1)
        best = None
        for c in range(chunks):
            kt = ktbuf[:, keys_of(c)]
            scores = jnp.dot(both, jnp.concatenate([kt, kt], axis=0), preferred_element_type=F32)
            sbuf[:, keys_of(c)] = scores
            for part in range(KEY_CHUNK // 128):
                piece = scores[:, part * 128 : (part + 1) * 128]
                best = piece if best is None else jnp.maximum(best, piece)
        row_max = jnp.max(best, axis=1, keepdims=True)
        total = jnp.zeros((ROWS, 2 * HEAD), F32)
        for c in range(chunks):
            weights = jnp.exp2(sbuf[:, keys_of(c)] - row_max).astype(BF16)
            slots = slice(c * KEY_CHUNK // TOK, (c + 1) * KEY_CHUNK // TOK)
            values = kvbuf[slots, 1].reshape(KEY_CHUNK, HEAD)
            total += jnp.dot(weights, jnp.concatenate([values, ones], axis=1), preferred_element_type=F32)
        attended = (total[:, :HEAD] * (value_scale / total[:, HEAD:])).astype(BF16)
        pairs = [
            jnp.concatenate([attended[k * TOK : k * TOK + LAT], attended[k * TOK + LAT : (k + 1) * TOK]], axis=1)
            for k in range(2)
        ]
        partial = jnp.dot(jnp.concatenate(pairs, axis=0), wblk[...], preferred_element_type=F32)
        partial = partial[:, :128] + partial[:, 128:]
        as_float = attended.astype(F32)
        square = as_float * as_float
        square_high = square.astype(BF16)
        square_low = (square - square_high.astype(F32)).astype(BF16)
        stats = lax.dot_general(
            picker,
            jnp.concatenate([attended, square_high, square_low], axis=1),
            (((1,), (1,)), ((), ())),
            preferred_element_type=F32,
        )[0:8]
        for k in range(2):
            pbuf[first + k, 0:LAT] = partial[k * LAT : (k + 1) * LAT]
            pbuf[first + k, LAT:PACK] = stats[:, k * TOK : (k + 1) * TOK] + consts[...]

    def one_group(g, _):
        with jax.named_scope("attend"):
            for half in range(2):
                for k in range(2):
                    j = g * NY + half * 2 + k

                    @pl.when(j < SEQ - 1)
                    def _():
                        q_copy(j).wait_recv()

                    @pl.when(j == SEQ - 1)
                    def _():
                        own_query.wait()

                attend(g * NY + half * 2)
            for i in range(NY - 1):
                y_copy(g, i).start()

        @pl.when(g > 0)
        def _():
            with jax.named_scope("join"):
                join_y(g - 1)
                z_copy(g - 1).start()

        return 0

    lax.fori_loop(0, NZ, one_group, 0)

    with jax.named_scope("tail"):
        join_y(NZ - 1)
        total = zsend[NZ - 1]
        for g in range(NZ - 1):
            z_copy(g).wait_recv()
            total = total + zbuf[g]

        center = total[LAT : LAT + 1] * (1.0 / WIDTH)
        spread = jnp.maximum(total[LAT + 1 : LAT + 2] * (1.0 / WIDTH) - center * center, 0.0)
        inverse = lax.rsqrt(spread + 1e-06)
        rows = lax.broadcasted_iota(jnp.int32, (128, 128), 0)
        stacked = jnp.where(rows == 0, inverse, jnp.where(rows == 1, center * inverse, 0.0)).T
        left = lax.broadcasted_iota(jnp.int32, (LAT, 128), 1) < LAT
        inverse_at = jnp.where(left, stacked[0:LAT, 0:1], stacked[LAT:, 0:1])
        center_at = jnp.where(left, stacked[0:LAT, 1:2], stacked[LAT:, 1:2])
        velocity = (
            inverse_at * total[0:LAT]
            - center_at * total[LAT + 2 : LAT + 3]
            + total[LAT + 3 : LAT + 4]
        )

        @pl.when(tm < TM - 1)
        def _():
            time_copy.wait_recv()

        @pl.when(tm == TM - 1)
        def _():
            later[1] = jnp.zeros((8, 128), F32)

        step = (later[1] - time_now) / 1000.0
        drift = velocity * step[0:1]
        tsend[...] = drift

        def t_copy(k):
            return pltpu.make_async_remote_copy(
                src_ref=tsend,
                dst_ref=tbuf.at[k - 1],
                send_sem=t_send.at[k - 1],
                recv_sem=t_recv.at[k - 1],
                device_id=((tm + k) % TM, me),
                device_id_type=MESH,
            )

        for k in range(1, TM):

            @pl.when(tm + k < TM)
            def _():
                t_copy(k).start()

        lat[0:LAT] = drift

        for k in range(1, TM):

            @pl.when(tm >= k)
            def _():
                t_copy(k).wait_recv()
                lat[0:LAT] += tbuf[k - 1]

        summed = lat[0:LAT]
        lat[LAT : 2 * LAT] = pltpu.roll(summed, LAT, 1)
        even = lat[pl.ds(0, LAT, stride=2)]
        odd = lat[pl.ds(1, LAT, stride=2)]
        out[...] = start_latent[...] + jnp.where(left, even, pltpu.roll(odd, LAT, 1))

    with jax.named_scope("drain"):

        def drain(j, _):
            kv_copy(j).wait_send()
            q_copy(j).wait_send()
            return 0

        lax.fori_loop(0, SEQ - 1, drain, 0)

        def drain_group(g, _):
            for i in range(NY - 1):
                y_copy(g, i).wait_send()

            @pl.when(g < NZ - 1)
            def _():
                z_copy(g).wait_send()

            return 0

        lax.fori_loop(0, NZ, drain_group, 0)
        for k in range(1, TM):

            @pl.when(tm + k < TM)
            def _():
                t_copy(k).wait_send()

        @pl.when(tm > 0)
        def _():
            time_copy.wait_send()


def body(projected, scale_table, group_index, timesteps, time_weight, head_weight, start_latent):
    codes = projected[0].transpose(1, 0, 2)
    table = scale_table.transpose(1, 0, 2)
    half = FREQ // 2
    values = np.power(np.float64(10000.0), -np.arange(half, dtype=np.float64) / half).astype(np.float32)
    freqs = jnp.asarray(np.repeat(np.concatenate([values, values]), 2)[None, :])
    any_space = pl.BlockSpec(memory_space=pl.ANY)
    vmem = pl.BlockSpec(memory_space=pltpu.VMEM)
    smem = pl.BlockSpec(memory_space=pltpu.SMEM)
    dma = pltpu.SemaphoreType.DMA
    latents = pl.pallas_call(
        kernel,
        name="window",
        out_shape=jax.ShapeDtypeStruct((LAT, 128), F32),
        in_specs=[any_space, vmem, smem, smem, vmem, any_space, any_space, vmem],
        out_specs=vmem,
        scratch_shapes=[
            pltpu.VMEM((SEQ, TOK, HEAD), BF16),
            pltpu.VMEM((SEQ, 2, TOK, HEAD), BF16),
            pltpu.VMEM((HEAD, KEYS), BF16),
            pltpu.VMEM((ROWS, KEYS), F32),
            pltpu.VMEM((2 * HEAD, 256), BF16),
            pltpu.VMEM((FREQ, 2, HEAD), BF16),
            pltpu.VMEM((LAT, HEAD), BF16),
            pltpu.VMEM((8, 128), F32),
            pltpu.VMEM((SEQ, PACK, 128), F32),
            pltpu.VMEM((SEQ, PACK, 128), F32),
            pltpu.VMEM((NZ, PACK, 128), F32),
            pltpu.VMEM((NZ, PACK, 128), F32),
            pltpu.VMEM((LAT, 128), F32),
            pltpu.VMEM((TM - 1, LAT, 128), F32),
            pltpu.VMEM((2, 8, 128), F32),
            pltpu.VMEM((2 * LAT, 128), F32),
            dma((SEQ,)),
            dma((SEQ,)),
            dma((SEQ,)),
            dma((SEQ,)),
            dma((SEQ,)),
            dma((SEQ,)),
            dma((NZ,)),
            dma((NZ,)),
            dma((TM - 1,)),
            dma((TM - 1,)),
            dma((6,)),
        ],
        compiler_params=pltpu.CompilerParams(
            collective_id=0, has_side_effects=True, vmem_limit_bytes=40 << 20
        ),
    )(codes, table, group_index, timesteps, freqs, time_weight, head_weight, start_latent)
    return latents[None]


def solution(mesh):
    placed = (P("tm", "seq", None, None), P(), P("tm"), P("tm"), P(), P(), P("seq", None))
    return jax.shard_map(
        body, mesh=mesh, in_specs=placed, out_specs=P("tm", "seq", None), check_vma=False
    )
```

time: 285 us -> 132 us (0.46)
  Pallas kernels: 0 us -> 123 us
  waiting for transfers between devices: 98.2 us -> 0 us
  other arithmetic: 47.9 us -> 0 us
  local copies, waits for them, and re-layouts: 43.7 us -> 7.87 us
  matrix products: 30.9 us -> 0 us
  starting transfers between devices: 24.3 us -> 0 us
  blocking collectives: 17.7 us -> 0 us
  loops' own time: 17 us -> 0 us
    pallas_call x0 -> x1, Pallas kernels: none -> 123 us  [body(): pl.pallas_call(kernel, name='window', out_shape=jax.ShapeDtypeStruct((LAT...]
    all_to_all x2 -> x0, waiting for transfers between devices: 98.2 us -> none  [the longest x1 90 us: body(): lax.all_to_all(projected, 'seq', split_axis=3, concat_axis=1, tiled=True)]
    dot_general x18 -> x0, matrix products: 30.9 us -> none  [the longest x8 16.8 us: one_block(): jnp.einsum('nhqk,nkhd->nqhd', weights.astype(jnp.bfloat16), value_codes,...]
    unnamed x2 -> x0, other arithmetic: 23.4 us -> none
    all_to_all x2 -> x0, starting transfers between devices: 20.7 us -> none  [the longest x1 11.5 us: body(): lax.all_to_all(projected, 'seq', split_axis=3, concat_axis=1, tiled=True)]
    all_gather x1 -> x0, blocking collectives: 17.7 us -> none  [entering(): everything = lax.all_gather(x, axis)]
    another operation x2 -> x0, loops' own time: 17 us -> none  [the longest x1 16.8 us: body(): pieces = lax.map(one_block, jnp.arange(length // block_rows) * block_rows)]
    unnamed x13, local copies, waits for them, and re-layouts: 22.3 us -> 7.87 us
  transfers between devices with their start and end apart: 3 -> 0, of which waited for: 2 -> 0; matrix products, arithmetic and copies ran while one was open for 4% -> 0% of each run, Pallas kernels for 0% -> 0%
where the time goes in v1:
time: 132 us
  Pallas kernels  123 us (93%)
  local copies, waits for them, and re-layouts  7.87 us (6%)
  between operations  1.32 us (1%)
    pallas_call x1, Pallas kernels, body(): pl.pallas_call(kernel, name='window', out_shape=jax.ShapeDtypeStruct((LAT...  123 us
    unnamed x13, local copies, waits for them, and re-layouts  7.87 us

profile of v1, /device:TPU:7, one launch (start us, length us, event | category | flops | bytes accessed | tf_op | source)
XLA Modules:
  0.0 131.9 jit_solution(640754494342481000)
XLA Ops:
  1.3 0.0 copy-start
  1.3 2.2 %copy-done = bf16[256,2,4096]{2,1,0:T(2,128)(2,1)S(1)} copy-done((bf16[256,2,4096]{2,1,0:T(2,128)(2,1)S(1)}, bf16[256,2,4096]{2,1,0:T(2,128)(2,1)}, u32[]{:S(2)}) %copy-start) | copy-done | bytes 4194328
  3.5 0.0 copy-start.1
  3.5 1.9 %copy-done.1 = bf16[1,128,3,4096]{3,1,2,0:T(8,128)(2,1)S(1)} copy-done((bf16[1,128,3,4096]{3,1,2,0:T(8,128)(2,1)S(1)}, bf16[1,128,3,4096]{3,1,2,0:T(8,128)(2,1)}, u32[]{:S(2)}) %copy-start.1) | copy-done | bytes 3145752
  5.4 0.0 copy-start.2
  5.4 1.0 copy-done.2
  6.4 0.0 copy-start.3
  6.4 0.8 copy-done.3
  7.2 0.0 copy-start.4
  7.2 0.7 copy-done.4
  7.9 0.0 copy-start.5
  7.9 0.7 copy-done.5
  8.6 122.7 %window.1 = f32[64,128]{1,0:T(8,128)S(1)} custom-call(bf16[3,128,4096]{2,1,0:T(8,128)(2,1)S(1)} %bitcast.5, f32[3,8,32]{2,1,0:T(8,128)S(1)} %bitcast.7, s32[1]{0:T(128)S(6)} %copy.10.group_index, s32[1]{0:T(128)S(6)} %copy.11.timesteps, f32[1,512]{1,0:T(1,128)S(1)} %copy-done.5, bf16[256,2,4096]{2,1,0:T(2,128)(2,1)S(1)} %copy-done, ...), custom_call_target="tpu_custom_call" | custom-call | tf_op jit(solution)/shard_map/window/pallas_call | solution.py:424
  131.2 0.6 copy.12
Async XLA Ops:
  1.3 2.2 %copy-start = (bf16[256,2,4096]{2,1,0:T(2,128)(2,1)S(1)}, bf16[256,2,4096]{2,1,0:T(2,128)(2,1)}, u32[]{:S(2)}) copy-start(bf16[256,2,4096]{2,1,0:T(2,128)(2,1)} %time_weight.1) | copy-start | bytes 12582916
  3.5 1.9 %copy-start.1 = (bf16[1,128,3,4096]{3,1,2,0:T(8,128)(2,1)S(1)}, bf16[1,128,3,4096]{3,1,2,0:T(8,128)(2,1)}, u32[]{:S(2)}) copy-start(bf16[1,128,3,4096]{3,1,2,0:T(8,128)(2,1)} %param.8) | copy-start | bytes 9437188
  5.4 1.0 copy-start.2
  6.4 0.8 copy-start.3
  7.2 0.7 copy-start.4
  7.9 0.7 copy-start.5

commit v2 on v1

--- a/solution.py
+++ b/solution.py
@@ -28,22 +28,26 @@
 
 def group_dz(g):
     odd = g % 2
-    return (4 + odd * ((g + 1) // 2) - (1 - odd) * (g // 2)) % NZ
+    return (odd * ((g + 1) // 2) - (1 - odd) * (g // 2)) % NZ
 
 
 def group_dy(i):
     return (i + 1) % NY
 
 
+OWN = NY - 1
+OTHERS = [j for j in range(SEQ) if j != OWN]
+
+
 def kernel(
     proj,
-    scale_table,
+    table_hbm,
     group_index,
     timesteps,
-    freqs,
+    freqs_hbm,
     time_weight,
     head_weight,
-    start_latent,
+    latent_hbm,
     out,
     qbuf,
     kvbuf,
@@ -53,6 +57,10 @@
     tw,
     hw,
     consts,
+    scale_table,
+    freqs,
+    start_latent,
+    mbuf,
     pbuf,
     ybuf,
     zsend,
@@ -84,8 +92,14 @@
         return (tm, seq_at(dy, dz))
 
     cols = pl.ds(pl.multiple_of(me * HEAD, HEAD), HEAD)
-    own_codes = pltpu.make_async_copy(proj.at[1:3, :, cols], kvbuf.at[SEQ - 1], misc.at[0])
-    own_query = pltpu.make_async_copy(proj.at[0, :, cols], qbuf.at[SEQ - 1], misc.at[1])
+    own_codes = pltpu.make_async_copy(proj.at[1:3, :, cols], kvbuf.at[OWN], misc.at[0])
+    own_query = pltpu.make_async_copy(proj.at[0, :, cols], qbuf.at[OWN], misc.at[1])
+    get_table = pltpu.make_async_copy(table_hbm, scale_table, misc.at[6])
+    get_freqs = pltpu.make_async_copy(freqs_hbm, freqs, misc.at[7])
+    get_latent = pltpu.make_async_copy(latent_hbm, start_latent, misc.at[8])
+    get_table.start()
+    get_freqs.start()
+    get_latent.start()
     get_tw = pltpu.make_async_copy(time_weight.at[:, :, cols], tw, misc.at[2])
     get_hw = pltpu.make_async_copy(head_weight.at[:, cols], hw, misc.at[3])
     own_codes.start()
@@ -134,17 +148,11 @@
             device_id_type=MESH,
         )
 
-    def start_kv(j, _):
-        kv_copy(j).start()
-        return 0
-
-    def start_q(j, _):
-        q_copy(j).start()
-        return 0
-
     with jax.named_scope("send"):
-        lax.fori_loop(0, SEQ - 1, start_kv, 0)
-        lax.fori_loop(0, SEQ - 1, start_q, 0)
+        for j in OTHERS:
+            kv_copy(j).start()
+        for j in OTHERS:
+            q_copy(j).start()
 
     time_copy = pltpu.make_async_remote_copy(
         src_ref=later.at[0],
@@ -162,7 +170,9 @@
         time_copy.start()
 
     with jax.named_scope("constants"):
-        lane = lax.broadcasted_iota(jnp.int32, (8, 128), 1)
+        get_table.wait()
+        get_freqs.wait()
+        get_latent.wait()
         row = lax.broadcasted_iota(jnp.int32, (8, 128), 0)
         head_lane = lax.broadcasted_iota(jnp.int32, (8, SEQ), 1)
         group_row = lax.broadcasted_iota(jnp.int32, (8, SEQ), 0)
@@ -200,16 +210,13 @@
         summed = jnp.sum(high.astype(F32) + low.astype(F32), axis=0, keepdims=True)
         consts[...] = jnp.where(row == 2, summed, jnp.where(row == 3, shifted, 0.0))
 
-    own_codes.wait()
-    ktbuf[:, KEYS - TOK : KEYS] = kvbuf[SEQ - 1, 0].T
-
-    def take_kv(j, _):
-        kv_copy(j).wait_recv()
-        ktbuf[:, pl.ds(pl.multiple_of(j * TOK, TOK), TOK)] = kvbuf[j, 0].T
-        return 0
-
     with jax.named_scope("keys"):
-        lax.fori_loop(0, SEQ - 1, take_kv, 0)
+        for j in range(SEQ):
+            if j == OWN:
+                own_codes.wait()
+            else:
+                kv_copy(j).wait_recv()
+            ktbuf[:, j * TOK : (j + 1) * TOK] = kvbuf[j, 0].T
 
     def y_copy(g, i):
         return pltpu.make_async_remote_copy(
@@ -247,26 +254,31 @@
         ((stat_row == 0) & (stat_lane < HEAD)) | ((stat_row == 1) & (stat_lane >= HEAD)), 1.0, 0.0
     ).astype(BF16)
 
-    def attend(first):
-        query = qbuf[pl.ds(first, 2)].reshape(ROWS, HEAD).astype(F32) * score_scale
+    def load_query(n):
+        query = qbuf[pl.ds(2 * n, 2)].reshape(ROWS, HEAD).astype(F32) * score_scale
         high = query.astype(BF16)
         low = (query - high.astype(F32)).astype(BF16)
-        both = jnp.concatenate([high, low], axis=1)
-        best = None
-        for c in range(chunks):
-            kt = ktbuf[:, keys_of(c)]
-            scores = jnp.dot(both, jnp.concatenate([kt, kt], axis=0), preferred_element_type=F32)
-            sbuf[:, keys_of(c)] = scores
-            for part in range(KEY_CHUNK // 128):
-                piece = scores[:, part * 128 : (part + 1) * 128]
-                best = piece if best is None else jnp.maximum(best, piece)
-        row_max = jnp.max(best, axis=1, keepdims=True)
-        total = jnp.zeros((ROWS, 2 * HEAD), F32)
-        for c in range(chunks):
-            weights = jnp.exp2(sbuf[:, keys_of(c)] - row_max).astype(BF16)
-            slots = slice(c * KEY_CHUNK // TOK, (c + 1) * KEY_CHUNK // TOK)
-            values = kvbuf[slots, 1].reshape(KEY_CHUNK, HEAD)
-            total += jnp.dot(weights, jnp.concatenate([values, ones], axis=1), preferred_element_type=F32)
+        return jnp.concatenate([high, low], axis=1)
+
+    def score(both, c, slot, best):
+        kt = ktbuf[:, keys_of(c)]
+        scores = jnp.dot(both, jnp.concatenate([kt, kt], axis=0), preferred_element_type=F32)
+        sbuf[slot, :, keys_of(c)] = scores
+        for part in range(KEY_CHUNK // 128):
+            piece = scores[:, part * 128 : (part + 1) * 128]
+            best = piece if best is None else jnp.maximum(best, piece)
+        return best
+
+    def keep_max(slot, best):
+        mbuf[slot] = jnp.broadcast_to(jnp.max(best, axis=1, keepdims=True), (ROWS, 128))
+
+    def blend(slot, c, row_max):
+        weights = jnp.exp2(sbuf[slot, :, keys_of(c)] - row_max).astype(BF16)
+        slots = slice(c * KEY_CHUNK // TOK, (c + 1) * KEY_CHUNK // TOK)
+        values = kvbuf[slots, 1].reshape(KEY_CHUNK, HEAD)
+        return jnp.dot(weights, jnp.concatenate([values, ones], axis=1), preferred_element_type=F32)
+
+    def finish(first, total):
         attended = (total[:, :HEAD] * (value_scale / total[:, HEAD:])).astype(BF16)
         pairs = [
             jnp.concatenate([attended[k * TOK : k * TOK + LAT], attended[k * TOK + LAT : (k + 1) * TOK]], axis=1)
@@ -288,29 +300,60 @@
             pbuf[first + k, 0:LAT] = partial[k * LAT : (k + 1) * LAT]
             pbuf[first + k, LAT:PACK] = stats[:, k * TOK : (k + 1) * TOK] + consts[...]
 
+    def block(n, slot):
+        both = load_query(jnp.minimum(n + 1, SEQ // 2 - 1))
+        row_max = mbuf[slot][:, 0:1]
+        best = None
+        total = jnp.zeros((ROWS, 2 * HEAD), F32)
+        for c in range(chunks):
+            best = score(both, c, 1 - slot, best)
+            total += blend(slot, c, row_max)
+        keep_max(1 - slot, best)
+        finish(2 * n, total)
+
+    with jax.named_scope("first"):
+        q_copy(0).wait_recv()
+        q_copy(1).wait_recv()
+        both = load_query(0)
+        best = None
+        for c in range(chunks):
+            best = score(both, c, 0, best)
+        keep_max(0, best)
+
     def one_group(g, _):
         with jax.named_scope("attend"):
-            for half in range(2):
-                for k in range(2):
-                    j = g * NY + half * 2 + k
-
-                    @pl.when(j < SEQ - 1)
-                    def _():
-                        q_copy(j).wait_recv()
-
-                    @pl.when(j == SEQ - 1)
-                    def _():
-                        own_query.wait()
-
-                attend(g * NY + half * 2)
-            for i in range(NY - 1):
-                y_copy(g, i).start()
+            q_copy(g * NY + 2).wait_recv()
+
+            @pl.when(g > 0)
+            def _():
+                q_copy(g * NY + 3).wait_recv()
+
+            @pl.when(g == 0)
+            def _():
+                own_query.wait()
+
+            block(2 * g, 0)
+            y_copy(g, 0).start()
+            y_copy(g, 1).start()
+
+        with jax.named_scope("attend"):
+
+            @pl.when(g < NZ - 1)
+            def _():
+                q_copy(g * NY + 4).wait_recv()
+                q_copy(g * NY + 5).wait_recv()
+
+            block(2 * g + 1, 1)
+            y_copy(g, 2).start()
 
         @pl.when(g > 0)
         def _():
             with jax.named_scope("join"):
                 join_y(g - 1)
-                z_copy(g - 1).start()
+
+                @pl.when(g > 1)
+                def _():
+                    z_copy(g - 1).start()
 
         return 0
 
@@ -318,8 +361,9 @@
 
     with jax.named_scope("tail"):
         join_y(NZ - 1)
-        total = zsend[NZ - 1]
-        for g in range(NZ - 1):
+        z_copy(NZ - 1).start()
+        total = zsend[0]
+        for g in range(1, NZ):
             z_copy(g).wait_recv()
             total = total + zbuf[g]
 
@@ -382,18 +426,15 @@
 
     with jax.named_scope("drain"):
 
-        def drain(j, _):
+        for j in OTHERS:
             kv_copy(j).wait_send()
             q_copy(j).wait_send()
-            return 0
-
-        lax.fori_loop(0, SEQ - 1, drain, 0)
 
         def drain_group(g, _):
             for i in range(NY - 1):
                 y_copy(g, i).wait_send()
 
-            @pl.when(g < NZ - 1)
+            @pl.when(g > 0)
             def _():
                 z_copy(g).wait_send()
 
@@ -425,17 +466,21 @@
         kernel,
         name="window",
         out_shape=jax.ShapeDtypeStruct((LAT, 128), F32),
-        in_specs=[any_space, vmem, smem, smem, vmem, any_space, any_space, vmem],
+        in_specs=[any_space, any_space, smem, smem, any_space, any_space, any_space, any_space],
         out_specs=vmem,
         scratch_shapes=[
             pltpu.VMEM((SEQ, TOK, HEAD), BF16),
             pltpu.VMEM((SEQ, 2, TOK, HEAD), BF16),
             pltpu.VMEM((HEAD, KEYS), BF16),
-            pltpu.VMEM((ROWS, KEYS), F32),
+            pltpu.VMEM((2, ROWS, KEYS), F32),
             pltpu.VMEM((2 * HEAD, 256), BF16),
             pltpu.VMEM((FREQ, 2, HEAD), BF16),
             pltpu.VMEM((LAT, HEAD), BF16),
             pltpu.VMEM((8, 128), F32),
+            pltpu.VMEM((3, 8, SEQ), F32),
+            pltpu.VMEM((1, 2 * FREQ), F32),
+            pltpu.VMEM((LAT, 128), F32),
+            pltpu.VMEM((2, ROWS, 128), F32),
             pltpu.VMEM((SEQ, PACK, 128), F32),
             pltpu.VMEM((SEQ, PACK, 128), F32),
             pltpu.VMEM((NZ, PACK, 128), F32),
@@ -454,10 +499,10 @@
             dma((NZ,)),
             dma((TM - 1,)),
             dma((TM - 1,)),
-            dma((6,)),
+            dma((9,)),
         ],
         compiler_params=pltpu.CompilerParams(
-            collective_id=0, has_side_effects=True, vmem_limit_bytes=40 << 20
+            collective_id=0, has_side_effects=True, vmem_limit_bytes=60 << 20
         ),
     )(codes, table, group_index, timesteps, freqs, time_weight, head_weight, start_latent)
     return latents[None]

time: 132 us -> 106 us (0.80)
  Pallas kernels: 123 us -> 103 us
  local copies, waits for them, and re-layouts: 7.87 us -> 1.38 us
    pallas_call x1, Pallas kernels: 123 us -> 103 us  [body(): pl.pallas_call(kernel, name='window', out_shape=jax.ShapeDtypeStruct((LAT...]
    unnamed x13 -> x1, local copies, waits for them, and re-layouts: 7.87 us -> 1.38 us
where the time goes in v2:
time: 106 us
  Pallas kernels  103 us (97%)
  local copies, waits for them, and re-layouts  1.38 us (1%)
  between operations  1.3 us (1%)
    pallas_call x1, Pallas kernels, body(): pl.pallas_call(kernel, name='window', out_shape=jax.ShapeDtypeStruct((LAT...  103 us

profile of v2, /device:TPU:7, one launch (start us, length us, event | category | flops | bytes accessed | tf_op | source)
XLA Modules:
  0.0 105.8 jit_solution(12733164391933727563)
XLA Ops:
  1.3 103.1 %window.1 = f32[64,128]{1,0:T(8,128)} custom-call(bf16[3,128,4096]{2,1,0:T(8,128)(2,1)} %bitcast.5, f32[3,8,32]{2,1,0:T(8,128)} %bitcast.7, s32[1]{0:T(128)S(6)} %copy.10.group_index, s32[1]{0:T(128)S(6)} %copy.11.timesteps, f32[1,512]{1,0:T(1,128)} %constant.2.clone.freqs_hbm, bf16[256,2,4096]{2,1,0:T(2,128)(2,1)} %time_weight.1, ...), custom_call_target="tpu_custom_call" | custom-call | tf_op jit(solution)/shard_map/window/pallas_call | solution.py:465
  104.4 1.4 %copy.12 = f32[1,64,128]{2,1,0:T(8,128)} copy(f32[1,64,128]{2,1,0:T(8,128)} %bitcast.6) | data formatting | bytes 65536

commit v3 on v2

--- a/solution.py
+++ b/solution.py
@@ -61,6 +61,7 @@
     freqs,
     start_latent,
     mbuf,
+    acc,
     pbuf,
     ybuf,
     zsend,
@@ -150,9 +151,13 @@
 
     with jax.named_scope("send"):
         for j in OTHERS:
+            if j < NY:
+                q_copy(j).start()
+        for j in OTHERS:
             kv_copy(j).start()
         for j in OTHERS:
-            q_copy(j).start()
+            if j >= NY:
+                q_copy(j).start()
 
     time_copy = pltpu.make_async_remote_copy(
         src_ref=later.at[0],
@@ -210,13 +215,6 @@
         summed = jnp.sum(high.astype(F32) + low.astype(F32), axis=0, keepdims=True)
         consts[...] = jnp.where(row == 2, summed, jnp.where(row == 3, shifted, 0.0))
 
-    with jax.named_scope("keys"):
-        for j in range(SEQ):
-            if j == OWN:
-                own_codes.wait()
-            else:
-                kv_copy(j).wait_recv()
-            ktbuf[:, j * TOK : (j + 1) * TOK] = kvbuf[j, 0].T
 
     def y_copy(g, i):
         return pltpu.make_async_remote_copy(
@@ -300,64 +298,94 @@
             pbuf[first + k, 0:LAT] = partial[k * LAT : (k + 1) * LAT]
             pbuf[first + k, LAT:PACK] = stats[:, k * TOK : (k + 1) * TOK] + consts[...]
 
-    def block(n, slot):
-        both = load_query(jnp.minimum(n + 1, SEQ // 2 - 1))
+    def block(n, slot, last=False):
+        both = None if last else load_query(n + 1)
         row_max = mbuf[slot][:, 0:1]
         best = None
         total = jnp.zeros((ROWS, 2 * HEAD), F32)
         for c in range(chunks):
-            best = score(both, c, 1 - slot, best)
+            if not last:
+                best = score(both, c, 1 - slot, best)
             total += blend(slot, c, row_max)
-        keep_max(1 - slot, best)
+        if not last:
+            keep_max(1 - slot, best)
         finish(2 * n, total)
 
+    def gather_step(n, c):
+        kt = ktbuf[:, keys_of(c)]
+        scores = jnp.dot(load_query(n), jnp.concatenate([kt, kt], axis=0), preferred_element_type=F32)
+        best = scores[:, 0:128]
+        for part in range(1, KEY_CHUNK // 128):
+            best = jnp.maximum(best, scores[:, part * 128 : (part + 1) * 128])
+        row_max = jnp.max(best, axis=1, keepdims=True)
+        if c > 0:
+            before = mbuf[n][:, 0:1]
+            row_max = jnp.maximum(before, row_max)
+        weights = jnp.exp2(scores - row_max).astype(BF16)
+        values = kvbuf[slice(c * NY, (c + 1) * NY), 1].reshape(KEY_CHUNK, HEAD)
+        total = jnp.dot(weights, jnp.concatenate([values, ones], axis=1), preferred_element_type=F32)
+        if c > 0:
+            total += acc[n] * jnp.exp2(before - row_max)
+        acc[n] = total
+        mbuf[n] = jnp.broadcast_to(row_max, (ROWS, 128))
+
+    with jax.named_scope("keys"):
+        for j in range(NY):
+            if j == OWN:
+                own_query.wait()
+            else:
+                q_copy(j).wait_recv()
+        for c in range(chunks):
+            for j in range(c * NY, (c + 1) * NY):
+                if j == OWN:
+                    own_codes.wait()
+                else:
+                    kv_copy(j).wait_recv()
+                ktbuf[:, j * TOK : (j + 1) * TOK] = kvbuf[j, 0].T
+            for n in range(2):
+                gather_step(n, c)
+        for n in range(2):
+            finish(2 * n, acc[n])
+        for i in range(NY - 1):
+            y_copy(0, i).start()
+
     with jax.named_scope("first"):
-        q_copy(0).wait_recv()
-        q_copy(1).wait_recv()
-        both = load_query(0)
+        q_copy(NY).wait_recv()
+        q_copy(NY + 1).wait_recv()
+        both = load_query(2)
         best = None
         for c in range(chunks):
             best = score(both, c, 0, best)
         keep_max(0, best)
 
-    def one_group(g, _):
+    def one_group(g, last=False):
         with jax.named_scope("attend"):
             q_copy(g * NY + 2).wait_recv()
-
-            @pl.when(g > 0)
-            def _():
-                q_copy(g * NY + 3).wait_recv()
-
-            @pl.when(g == 0)
-            def _():
-                own_query.wait()
-
+            q_copy(g * NY + 3).wait_recv()
             block(2 * g, 0)
             y_copy(g, 0).start()
             y_copy(g, 1).start()
-
-        with jax.named_scope("attend"):
-
-            @pl.when(g < NZ - 1)
-            def _():
+            if not last:
                 q_copy(g * NY + 4).wait_recv()
                 q_copy(g * NY + 5).wait_recv()
-
-            block(2 * g + 1, 1)
+            block(2 * g + 1, 1, last)
             y_copy(g, 2).start()
 
-        @pl.when(g > 0)
-        def _():
-            with jax.named_scope("join"):
-                join_y(g - 1)
-
-                @pl.when(g > 1)
-                def _():
-                    z_copy(g - 1).start()
+    def each_group(g, _):
+        one_group(g)
+        with jax.named_scope("join"):
+            join_y(g - 1)
+
+            @pl.when(g > 1)
+            def _():
+                z_copy(g - 1).start()
 
         return 0
 
-    lax.fori_loop(0, NZ, one_group, 0)
+    lax.fori_loop(1, NZ - 1, each_group, 0)
+    one_group(NZ - 1, True)
+    join_y(NZ - 2)
+    z_copy(NZ - 2).start()
 
     with jax.named_scope("tail"):
         join_y(NZ - 1)
@@ -465,7 +493,7 @@
     latents = pl.pallas_call(
         kernel,
         name="window",
-        out_shape=jax.ShapeDtypeStruct((LAT, 128), F32),
+        out_shape=pltpu.VMEM((LAT, 128), F32),
         in_specs=[any_space, any_space, smem, smem, any_space, any_space, any_space, any_space],
         out_specs=vmem,
         scratch_shapes=[
@@ -481,6 +509,7 @@
             pltpu.VMEM((1, 2 * FREQ), F32),
             pltpu.VMEM((LAT, 128), F32),
             pltpu.VMEM((2, ROWS, 128), F32),
+            pltpu.VMEM((2, ROWS, 2 * HEAD), F32),
             pltpu.VMEM((SEQ, PACK, 128), F32),
             pltpu.VMEM((SEQ, PACK, 128), F32),
             pltpu.VMEM((NZ, PACK, 128), F32),

time: 106 us -> 104 us (0.981)
  no operation moved by 1% of the time
where the time goes in v3:
time: 104 us
  Pallas kernels  102 us (98%)
  between operations  1.31 us (1%)
    pallas_call x1, Pallas kernels, body(): pl.pallas_call(kernel, name='window', out_shape=pltpu.VMEM((LAT, 128), F3...  102 us

profile of v3, /device:TPU:7, one launch (start us, length us, event | category | flops | bytes accessed | tf_op | source)
XLA Modules:
  0.0 104.1 jit_solution(6245727206373959233)
XLA Ops:
  1.3 102.2 %window.1 = f32[64,128]{1,0:T(8,128)S(1)} custom-call(bf16[3,128,4096]{2,1,0:T(8,128)(2,1)} %bitcast.6, f32[3,8,32]{2,1,0:T(8,128)} %bitcast.7, s32[1]{0:T(128)S(6)} %copy.11.group_index, s32[1]{0:T(128)S(6)} %copy.12.timesteps, f32[1,512]{1,0:T(1,128)} %constant.2.clone.freqs_hbm, bf16[256,2,4096]{2,1,0:T(2,128)(2,1)} %time_weight.1, ...), custom_call_target="tpu_custom_call" | custom-call | tf_op jit(solution)/shard_map/window/pallas_call | solution.py:493
  103.5 0.6 copy.10

commit v4 on v3

--- a/solution.py
+++ b/solution.py
@@ -390,6 +390,9 @@
     with jax.named_scope("tail"):
         join_y(NZ - 1)
         z_copy(NZ - 1).start()
+        for j in OTHERS:
+            kv_copy(j).wait_send()
+            q_copy(j).wait_send()
         total = zsend[0]
         for g in range(1, NZ):
             z_copy(g).wait_recv()
@@ -437,6 +440,17 @@
             def _():
                 t_copy(k).start()
 
+        def drain_group(g, _):
+            for i in range(NY - 1):
+                y_copy(g, i).wait_send()
+
+            @pl.when(g > 0)
+            def _():
+                z_copy(g).wait_send()
+
+            return 0
+
+        lax.fori_loop(0, NZ, drain_group, 0)
         lat[0:LAT] = drift
 
         for k in range(1, TM):
@@ -454,21 +468,7 @@
 
     with jax.named_scope("drain"):
 
-        for j in OTHERS:
-            kv_copy(j).wait_send()
-            q_copy(j).wait_send()
-
-        def drain_group(g, _):
-            for i in range(NY - 1):
-                y_copy(g, i).wait_send()
-
-            @pl.when(g > 0)
-            def _():
-                z_copy(g).wait_send()
-
-            return 0
-
-        lax.fori_loop(0, NZ, drain_group, 0)
+
         for k in range(1, TM):
 
             @pl.when(tm + k < TM)

time: 104 us -> 104 us (level)
  no operation moved by 1% of the time
where the time goes in v4:
time: 104 us
  Pallas kernels  102 us (98%)
  between operations  1.31 us (1%)
    pallas_call x1, Pallas kernels, body(): pl.pallas_call(kernel, name='window', out_shape=pltpu.VMEM((LAT, 128), F3...  102 us

profile of v4, /device:TPU:7, one launch (start us, length us, event | category | flops | bytes accessed | tf_op | source)
XLA Modules:
  0.0 103.9 jit_solution(15280350388038896854)
XLA Ops:
  1.3 102.0 %window.1 = f32[64,128]{1,0:T(8,128)S(1)} custom-call(bf16[3,128,4096]{2,1,0:T(8,128)(2,1)} %bitcast.6, f32[3,8,32]{2,1,0:T(8,128)} %bitcast.7, s32[1]{0:T(128)S(6)} %copy.11.group_index, s32[1]{0:T(128)S(6)} %copy.12.timesteps, f32[1,512]{1,0:T(1,128)} %constant.2.clone.freqs_hbm, bf16[256,2,4096]{2,1,0:T(2,128)(2,1)} %time_weight.1, ...), custom_call_target="tpu_custom_call" | custom-call | tf_op jit(solution)/shard_map/window/pallas_call | solution.py:493
  103.3 0.6 copy.10
